TPU v7x, 32 devices: a whole 2x2x4 slice. The times are simulated.
32 devices in a mesh: dp: 8 (over y, x, core), seq: 4 (over z).
Axes of the slice: x: 2, y: 2, z: 4, core: 2. Of those that a mesh axis runs over, the one named last changes fastest.
Arguments:
- queries: bfloat16 [8, 512, 4096], P('dp', 'seq'), may hold values from -512 to 512
- key_rows: bfloat16 [8, 512, 4096], P('dp', 'seq'), may hold values from -18 to 18
- value_rows: bfloat16 [8, 512, 4096], P('dp', 'seq'), may hold values from -6 to 6
- w_out: bfloat16 [4096, 3072], P('seq', 'dp'), may hold values from -1.5 to 1.5
Outputs:
- attn_output: bfloat16 [8, 512, 3072], P('dp', 'seq')
All inputs are finite; a program needn't handle non-finite values.
Results may differ from a plain program's by a relative error of at most 0.0095.
Values may be sent and summed in bfloat16 or wider, within the bound.
A program may use at most 128 MiB of HBM per device.

v0:
```python
import jax
import jax.numpy as jnp
from jax import lax
from jax.sharding import PartitionSpec as P

HEAD_DIM = 128


def attend_block(qblock, keys_all, values_all, factor):
    scores = (
        jnp.einsum("qhd,khd->hqk", qblock, keys_all, preferred_element_type=jnp.float32) * factor
    )
    largest = jnp.max(scores, axis=2, keepdims=True)
    weights = jnp.exp(scores - largest)
    totals = jnp.sum(weights, axis=2, keepdims=True)
    probs = (weights / totals).astype(jnp.bfloat16)
    mixed = jnp.einsum("hqk,khd->qhd", probs, values_all, preferred_element_type=jnp.float32)
    return mixed.astype(jnp.bfloat16)


def attention(triple):
    queries, keys_all, values_all = triple
    length = queries.shape[0]
    number = queries.shape[2]
    factor = HEAD_DIM ** (-0.5)
    block = min(512, length)
    blocked = queries.reshape(length // block, block, number, HEAD_DIM)
    keys_flat = keys_all.reshape(length, number, HEAD_DIM)
    values_flat = values_all.reshape(length, number, HEAD_DIM)
    outcome = lax.map(lambda qblock: attend_block(qblock, keys_flat, values_flat, factor), blocked)
    return outcome.reshape(length, 1, number, HEAD_DIM)


def per_device(queries, key_rows, value_rows, w_out):
    tokens = queries.shape[1]
    width = queries.shape[2]
    heads = width // HEAD_DIM
    groups = lax.axis_size("seq")
    per_group = heads // groups
    query_heads = queries.reshape(tokens, groups, per_group, HEAD_DIM)
    key_heads = key_rows.reshape(tokens, groups, per_group, HEAD_DIM)
    value_heads = value_rows.reshape(tokens, groups, per_group, HEAD_DIM)
    attended = attention(
        (
            lax.all_to_all(query_heads, "seq", split_axis=1, concat_axis=0, tiled=True),
            lax.all_to_all(key_heads, "seq", split_axis=1, concat_axis=0, tiled=True),
            lax.all_to_all(value_heads, "seq", split_axis=1, concat_axis=0, tiled=True),
        )
    )
    length = attended.shape[0]
    local_heads = attended.reshape(length, per_group * HEAD_DIM)
    weight_heads = lax.all_gather(w_out, "dp", axis=1, tiled=True)
    output = lax.psum_scatter(
        jnp.dot(local_heads, weight_heads, preferred_element_type=jnp.float32).astype(jnp.bfloat16),
        "seq",
        scatter_dimension=0,
        tiled=True,
    )
    return output.reshape(1, tokens, output.shape[1])


def solution(mesh):
    in_specs = (P("dp", "seq", None), P("dp", "seq", None), P("dp", "seq", None), P("seq", "dp"))
    out_specs = P("dp", "seq", None)
    return jax.shard_map(
        per_device, mesh=mesh, in_specs=in_specs, out_specs=out_specs, check_vma=False
    )
```

profile of v0, /device:TPU:10, one launch (start us, length us, event | category | flops | bytes accessed | tf_op | source)
XLA Modules:
  0.0 184.5 jit_solution(633345587022387854)
XLA Ops:
  6.5 0.0 copy-start
  6.5 0.0 all-gather.2.cloned.1.call-start
  6.5 0.7 all-gather.2.cloned.1.call-update
  7.3 1.6 copy.14
  8.9 1.3 copy.15
  10.2 5.3 %all-to-all-start = ((bf16[128,4,8,128]{3,0,2,1:T(8,128)(2,1)}), bf16[128,4,8,128]{3,0,2,1:T(8,128)(2,1)S(1)}, u32[]{:S(2)}, u32[]{:S(2)}) async-start(bf16[128,4,8,128]{3,0,2,1:T(8,128)(2,1)} %copy.15), calls=%async_computation | async-start | bytes 2097152 | tf_op jit(solution)/shard_map/all_to_all | solution.py:45
  15.5 1.6 copy.17
  17.1 1.3 copy.18
  18.5 19.5 %all-to-all-done = bf16[128,4,8,128]{3,0,2,1:T(8,128)(2,1)S(1)} async-done(((bf16[128,4,8,128]{3,0,2,1:T(8,128)(2,1)}), bf16[128,4,8,128]{3,0,2,1:T(8,128)(2,1)S(1)}, u32[]{:S(2)}, u32[]{:S(2)}) %all-to-all-start) | async-done | bytes 1048608 | tf_op jit(solution)/shard_map/all_to_all | solution.py:45
  38.0 6.8 %all-to-all-start.1 = ((bf16[128,4,8,128]{3,0,2,1:T(8,128)(2,1)}), bf16[128,4,8,128]{3,0,2,1:T(8,128)(2,1)S(1)}, u32[]{:S(2)}, u32[]{:S(2)}) async-start(bf16[128,4,8,128]{3,0,2,1:T(8,128)(2,1)} %copy.18), calls=%async_computation.1 | async-start | bytes 2097152 | tf_op jit(solution)/shard_map/all_to_all | solution.py:46
  44.7 0.0 copy-done
  44.7 1.3 copy.20
  46.0 20.7 %all-to-all-done.1 = bf16[128,4,8,128]{3,0,2,1:T(8,128)(2,1)S(1)} async-done(((bf16[128,4,8,128]{3,0,2,1:T(8,128)(2,1)}), bf16[128,4,8,128]{3,0,2,1:T(8,128)(2,1)S(1)}, u32[]{:S(2)}, u32[]{:S(2)}) %all-to-all-start.1) | async-done | bytes 1048608 | tf_op jit(solution)/shard_map/all_to_all | solution.py:46
  66.7 6.8 %all-to-all-start.2 = ((bf16[128,4,8,128]{0,3,2,1:T(8,128)(2,1)}), bf16[128,4,8,128]{0,3,2,1:T(8,128)(2,1)S(1)}, u32[]{:S(2)}, u32[]{:S(2)}) async-start(bf16[128,4,8,128]{0,3,2,1:T(8,128)(2,1)} %bitcast.8), calls=%async_computation.2 | async-start | bytes 2097152 | tf_op jit(solution)/shard_map/all_to_all | solution.py:47
  73.4 0.0 reduce-scatter.2.cloned.1.call-start
  73.4 1.1 copy.16
  74.5 1.1 copy.19
  75.6 19.8 %all-to-all-done.2 = bf16[128,4,8,128]{0,3,2,1:T(8,128)(2,1)S(1)} async-done(((bf16[128,4,8,128]{0,3,2,1:T(8,128)(2,1)}), bf16[128,4,8,128]{0,3,2,1:T(8,128)(2,1)S(1)}, u32[]{:S(2)}, u32[]{:S(2)}) %all-to-all-start.2) | async-done | bytes 1048608 | tf_op jit(solution)/shard_map/all_to_all | solution.py:47
  95.4 0.8 copy.21
  96.2 0.4 reshape.30
  96.7 7.5 %fusion.10 = (f32[8,512]{1,0:T(8,128)S(1)}, f32[8,512,512]{1,2,0:T(8,128)}) fusion(bf16[512,8,128]{2,0,1:T(8,128)(2,1)} %bitcast.32, bf16[512,8,128]{2,0,1:T(8,128)(2,1)} %bitcast.33), kind=kOutput, calls=%fused_computation.11 | convolution fusion | flops 543162880 | bytes 10502144 | tf_op jit(solution)/shard_map/while/body/eval_jaxpr/sub | solution.py:14
  104.1 4.1 %fusion.6 = bf16[8,512,128]{1,2,0:T(8,128)(2,1)S(1)} fusion(bf16[512,8,128]{0,2,1:T(8,128)(2,1)S(1)} %reshape.30, f32[8,512,512]{1,2,0:T(8,128)} %get-tuple-element.14, f32[8,512]{1,0:T(8,128)S(1)} %get-tuple-element.13), kind=kOutput, calls=%fused_computation.8 | convolution fusion | flops 541589504 | bytes 10502144 | tf_op jit(solution)/shard_map/while/body/eval_jaxpr/hqk,khd->qhd/dot_general | solution.py:17
  108.2 0.0 all-gather.2.cloned.1.call-done
  108.3 7.6 %convolution_convert_fusion = bf16[512,3072]{1,0:T(8,128)(2,1)} fusion(bf16[512,1024]{0,1:T(8,128)(2,1)S(1)} %bitcast.34, bf16[1024,3072]{1,0:T(8,128)(2,1)} %all-gather.2.cloned.1.call-done), kind=kOutput, calls=%fused_computation.5 | convolution fusion | flops 3222798336 | bytes 10485760 | tf_op jit(solution)/shard_map/dot_general | solution.py:54
  115.9 0.0 reduce-scatter.2.cloned.1.call-update
  115.9 61.8 %reduce-scatter.2.cloned.1.call-done = bf16[128,3072]{1,0:T(8,128)(2,1)} async-done(((bf16[512,3072]{1,0:T(8,128)(2,1)}), bf16[128,3072]{1,0:T(8,128)(2,1)}) %reduce-scatter.2.cloned.1.call-update) | async-done | bytes 786448 | tf_op jit(solution)/shard_map/reduce_scatter | solution.py:53
Async XLA Ops:
  6.5 38.2 %copy-start = (bf16[1,128,4096]{2,1,0:T(8,128)(2,1)S(1)}, bf16[1,128,4096]{2,1,0:T(8,128)(2,1)}, u32[]{:S(2)}) copy-start(bf16[1,128,4096]{2,1,0:T(8,128)(2,1)} %param.6) | copy-start | bytes 3145732
  6.5 101.7 %all-gather.2.cloned.1.call-start = ((), (), s32[]{:S(2)}) async-start(), calls=%async_computation.4 | async-start | bytes 7077888 | tf_op jit(solution)/shard_map/all_gather | solution.py:52
  10.2 27.8 %all-to-all-start = ((bf16[128,4,8,128]{3,0,2,1:T(8,128)(2,1)}), bf16[128,4,8,128]{3,0,2,1:T(8,128)(2,1)S(1)}, u32[]{:S(2)}, u32[]{:S(2)}) async-start(bf16[128,4,8,128]{3,0,2,1:T(8,128)(2,1)} %copy.15), calls=%async_computation | async-start | bytes 2097152 | tf_op jit(solution)/shard_map/all_to_all | solution.py:45
  38.0 28.7 %all-to-all-start.1 = ((bf16[128,4,8,128]{3,0,2,1:T(8,128)(2,1)}), bf16[128,4,8,128]{3,0,2,1:T(8,128)(2,1)S(1)}, u32[]{:S(2)}, u32[]{:S(2)}) async-start(bf16[128,4,8,128]{3,0,2,1:T(8,128)(2,1)} %copy.18), calls=%async_computation.1 | async-start | bytes 2097152 | tf_op jit(solution)/shard_map/all_to_all | solution.py:46
  66.7 28.7 %all-to-all-start.2 = ((bf16[128,4,8,128]{0,3,2,1:T(8,128)(2,1)}), bf16[128,4,8,128]{0,3,2,1:T(8,128)(2,1)S(1)}, u32[]{:S(2)}, u32[]{:S(2)}) async-start(bf16[128,4,8,128]{0,3,2,1:T(8,128)(2,1)} %bitcast.8), calls=%async_computation.2 | async-start | bytes 2097152 | tf_op jit(solution)/shard_map/all_to_all | solution.py:47
  73.4 104.2 %reduce-scatter.2.cloned.1.call-start = ((), (), s32[]{:S(2)}) async-start(), calls=%async_computation.5 | async-start | bytes 3932160 | tf_op jit(solution)/shard_map/reduce_scatter | solution.py:53
Sparse Core Ops, SparseCore 0:
  9.2 47.7 all-gather.1
  116.0 61.5 reduce-scatter.1
where the time goes:
time: 187 us; the launch traced here: 185 us
  waiting for transfers between devices  122 us (65%)
  matrix products  19.2 us (10%)
  starting transfers between devices  18.8 us (10%)
  between operations  13.4 us (7%)
  local copies, waits for them, and re-layouts  10.6 us (6%)
    reduce_scatter x1, waiting for transfers between devices, per_device(): lax.psum_scatter(jnp.dot(local_heads, weight_heads, preferred_element_typ...  61.8 us
    all_to_all x1, waiting for transfers between devices, per_device(): lax.all_to_all(key_heads, 'seq', split_axis=1, concat_axis=0, tiled=True)  20.7 us
    all_to_all x1, waiting for transfers between devices, per_device(): lax.all_to_all(value_heads, 'seq', split_axis=1, concat_axis=0, tiled=True)  19.8 us
    all_to_all x1, waiting for transfers between devices, per_device(): lax.all_to_all(query_heads, 'seq', split_axis=1, concat_axis=0, tiled=True)  19.5 us
    dot_general x1, matrix products, per_device(): jnp.dot(local_heads, weight_heads, preferred_element_type=jnp.float32)  7.64 us
    sub x1, matrix products, attend_block(): weights = jnp.exp(scores - largest)  7.46 us
    all_to_all x1, starting transfers between devices, per_device(): lax.all_to_all(value_heads, 'seq', split_axis=1, concat_axis=0, tiled=True)  6.76 us
    all_to_all x1, starting transfers between devices, per_device(): lax.all_to_all(key_heads, 'seq', split_axis=1, concat_axis=0, tiled=True)  6.76 us
  transfers between devices with their start and end apart: 5, of which 4 were waited for; matrix products, arithmetic and copies ran while one was open for 12% of the time, Pallas kernels for 0%

commit v1 on v0

v1 whole, which is shorter than its diff:
```python
import functools
import math

import jax
import jax.numpy as jnp
from jax import lax
from jax.experimental import pallas as pl
from jax.experimental.pallas import tpu as pltpu
from jax.sharding import PartitionSpec as P

HEAD_DIM = 128


def kernel(n, m, q_in, k_in, v_in, w_in, out, qb, kb, vb, wb, att, part, inbox,
           own_sem, qkv_send, qkv_recv, w_send, w_recv, sum_send, sum_recv):
    me = lax.axis_index("seq")
    col = lax.axis_index("dp")
    tokens = q_in.shape[0]
    feats = q_in.shape[1] // n
    heads = feats // HEAD_DIM
    length = tokens * n
    wcols = w_in.shape[1]

    def seq_peer(off):
        return lax.rem(me + off, n)

    def dp_peer(off):
        return lax.rem(col + off, m)

    barrier = pltpu.get_barrier_semaphore()
    for off in range(1, n):
        pl.semaphore_signal(barrier, inc=1, device_id={"seq": seq_peer(off)},
                            device_id_type=pl.DeviceIdType.MESH)
    for off in range(1, m):
        pl.semaphore_signal(barrier, inc=1, device_id={"dp": dp_peer(off)},
                            device_id_type=pl.DeviceIdType.MESH)
    pl.semaphore_wait(barrier, n + m - 2)

    trio = ((k_in, kb), (v_in, vb), (q_in, qb))

    def rows(dev):
        return pl.ds(pl.multiple_of(dev * tokens, tokens), tokens)

    def cols(dev):
        return pl.ds(pl.multiple_of(dev * feats, feats), feats)

    def qkv_copy(t, off):
        src, dst = trio[t]
        return pltpu.make_async_remote_copy(
            src_ref=src.at[:, cols(seq_peer(off))], dst_ref=dst.at[rows(me)],
            send_sem=qkv_send.at[t, off], recv_sem=qkv_recv.at[t, off],
            device_id={"seq": seq_peer(off)}, device_id_type=pl.DeviceIdType.MESH)

    def qkv_arrival(t, off):
        src, dst = trio[t]
        return pltpu.make_async_remote_copy(
            src_ref=src.at[:, cols(me)], dst_ref=dst.at[rows(lax.rem(me + n - off, n))],
            send_sem=qkv_send.at[t, off], recv_sem=qkv_recv.at[t, off],
            device_id={"seq": seq_peer(1)}, device_id_type=pl.DeviceIdType.MESH)

    def w_copy(off):
        return pltpu.make_async_remote_copy(
            src_ref=w_in, dst_ref=wb.at[col],
            send_sem=w_send.at[off], recv_sem=w_recv.at[off],
            device_id={"dp": dp_peer(off)}, device_id_type=pl.DeviceIdType.MESH)

    def w_arrival(off):
        return pltpu.make_async_remote_copy(
            src_ref=w_in, dst_ref=wb.at[lax.rem(col + m - off, m)],
            send_sem=w_send.at[off], recv_sem=w_recv.at[off],
            device_id={"dp": dp_peer(1)}, device_id_type=pl.DeviceIdType.MESH)

    for t in range(3):
        for off in range(1, n):
            qkv_copy(t, off).start()
    for off in range(1, m):
        w_copy(off).start()
    own = [pltpu.make_async_copy(trio[t][0].at[:, cols(me)], trio[t][1].at[rows(me)], own_sem.at[t])
           for t in range(3)]
    own.append(pltpu.make_async_copy(w_in, wb.at[col], own_sem.at[3]))
    for copy in own:
        copy.start()
    for copy in own:
        copy.wait()
    for t in range(2):
        for off in range(1, n):
            qkv_arrival(t, off).wait_recv()

    scale = HEAD_DIM ** -0.5 * math.log2(math.e)

    def attend(dest):
        for h in range(heads):
            c = slice(h * HEAD_DIM, (h + 1) * HEAD_DIM)
            s = lax.dot_general(qb[rows(dest), c], kb[:, c], (((1,), (1,)), ((), ())),
                                preferred_element_type=jnp.float32)
            top = jnp.max(s, axis=1, keepdims=True)
            p = jnp.exp2((s - top) * scale)
            total = jnp.sum(p, axis=1, keepdims=True)
            o = jnp.dot(p.astype(jnp.bfloat16), vb[:, c], preferred_element_type=jnp.float32)
            att[:, c] = (o / total).astype(jnp.bfloat16)

    def project(dest):
        for j in range(m):
            part[dest, :, j * wcols:(j + 1) * wcols] = jnp.dot(
                att[...], wb[j], preferred_element_type=jnp.float32).astype(jnp.bfloat16)

    def sum_copy(dest, up):
        target = me + 2 * up - 1
        slot = jnp.where((up == 0) & (target == dest), n, dest)
        return pltpu.make_async_remote_copy(
            src_ref=part.at[dest], dst_ref=inbox.at[slot],
            send_sem=sum_send.at[dest], recv_sem=sum_recv.at[slot],
            device_id={"seq": target}, device_id_type=pl.DeviceIdType.MESH)

    def sum_arrival(slot):
        return pltpu.make_async_remote_copy(
            src_ref=part.at[0], dst_ref=inbox.at[slot],
            send_sem=sum_send.at[0], recv_sem=sum_recv.at[slot],
            device_id={"seq": seq_peer(1)}, device_id_type=pl.DeviceIdType.MESH)

    low = jnp.where(me < n // 2, 1, 0)

    def item(index, carry):
        s = index // 2
        pos = index % 2
        up = jnp.where(pos == 0, low, 1 - low)
        dest = jnp.where(up == 1, n - 1 - s, s)

        @pl.when(s < (n + 1) // 2)
        def _():
            @pl.when(dest != me)
            def _():
                qkv_arrival(2, lax.rem(me - dest + n, n)).wait_recv()

            attend(dest)

            @pl.when(index == 0)
            def _():
                for off in range(1, m):
                    w_arrival(off).wait_recv()

            project(dest)

        active = jnp.where(up == 1, jnp.where(me < dest, 1, 0), jnp.where(me > dest, 1, 0))
        inner = jnp.where(up == 1, jnp.where(me > 0, 1, 0), jnp.where(me < n - 1, 1, 0))

        @pl.when(active == 1)
        def _():
            @pl.when(inner == 1)
            def _():
                sum_arrival(dest).wait_recv()
                part[dest] = (part[dest].astype(jnp.float32)
                              + inbox[dest].astype(jnp.float32)).astype(jnp.bfloat16)

            sum_copy(dest, up).start()

        return carry

    lax.fori_loop(0, 2 * n, item, 0)

    @pl.when(me > 0)
    def _():
        sum_arrival(me).wait_recv()

    @pl.when(me < n - 1)
    def _():
        sum_arrival(n).wait_recv()

    @pl.when(me == 0)
    def _():
        out[...] = (part[me].astype(jnp.float32) + inbox[n].astype(jnp.float32)).astype(jnp.bfloat16)

    @pl.when(me == n - 1)
    def _():
        out[...] = (part[me].astype(jnp.float32) + inbox[me].astype(jnp.float32)).astype(jnp.bfloat16)

    @pl.when((me > 0) & (me < n - 1))
    def _():
        out[...] = (part[me].astype(jnp.float32) + inbox[me].astype(jnp.float32)
                    + inbox[n].astype(jnp.float32)).astype(jnp.bfloat16)

    for t in range(3):
        for off in range(1, n):
            qkv_copy(t, off).wait_send()
    for off in range(1, m):
        w_copy(off).wait_send()

    def drain(dest, carry):
        @pl.when(dest != me)
        def _():
            sum_copy(dest, jnp.where(dest > me, 1, 0)).wait_send()
        return carry

    lax.fori_loop(0, n, drain, 0)


def per_device(n, m, queries, key_rows, value_rows, w_out):
    tokens, width = queries.shape[1:]
    depth, wcols = w_out.shape
    feats = width // n
    length = tokens * n
    dout = wcols * m
    bf16 = jnp.bfloat16
    vmem = pltpu.VMEM
    dma = pltpu.SemaphoreType.DMA
    flat = [a.reshape(tokens, width) for a in (queries, key_rows, value_rows)]
    result = pl.pallas_call(
        functools.partial(kernel, n, m),
        out_shape=jax.ShapeDtypeStruct((tokens, dout), bf16),
        in_specs=[pl.BlockSpec(memory_space=pl.ANY)] * 4,
        out_specs=pl.BlockSpec(memory_space=vmem),
        scratch_shapes=[
            vmem((length, feats), bf16), vmem((length, feats), bf16), vmem((length, feats), bf16),
            vmem((m, depth, wcols), bf16), vmem((tokens, feats), bf16),
            vmem((n, tokens, dout), bf16), vmem((n + 1, tokens, dout), bf16),
            dma((4,)), dma((3, n)), dma((3, n)), dma((m,)), dma((m,)), dma((n,)), dma((n + 1,)),
        ],
        compiler_params=pltpu.CompilerParams(
            collective_id=0, has_side_effects=True, vmem_limit_bytes=56 * 1024 * 1024),
        cost_estimate=pl.CostEstimate(
            flops=4 * length * length * feats + 2 * length * feats * dout,
            bytes_accessed=2 * (3 * tokens * width + depth * wcols),
            transcendentals=length * length * feats // HEAD_DIM),
    )(*flat, w_out)
    return result.reshape(1, tokens, dout)


def solution(mesh):
    n, m = mesh.shape["seq"], mesh.shape["dp"]
    in_specs = (P("dp", "seq", None), P("dp", "seq", None), P("dp", "seq", None), P("seq", "dp"))
    out_specs = P("dp", "seq", None)
    return jax.shard_map(
        functools.partial(per_device, n, m), mesh=mesh, in_specs=in_specs, out_specs=out_specs,
        check_vma=False
    )
```

time: 187 us -> 130 us (0.70)
  the two profiles are of different devices: /device:TPU:10 before, /device:TPU:9 now
where the time goes in v1:
time: 130 us
  Pallas kernels  128 us (98%)
  local copies, waits for them, and re-layouts  2.06 us (2%)
    pallas_call x1, Pallas kernels, per_device(): pl.pallas_call(functools.partial(kernel, n, m), out_shape=jax.ShapeDtypeS...  128 us

profile of v1, /device:TPU:9, one launch (start us, length us, event | category | flops | bytes accessed | tf_op | source)
XLA Modules:
  0.0 129.6 jit_solution(12918845278380950238)
XLA Ops:
  0.0 127.5 %shard_map.46 = bf16[128,3072]{1,0:T(8,128)(2,1)} custom-call(bf16[128,4096]{1,0:T(8,128)(2,1)} %bitcast.5, bf16[128,4096]{1,0:T(8,128)(2,1)} %bitcast.6, bf16[128,4096]{1,0:T(8,128)(2,1)} %bitcast.7, bf16[1024,384]{1,0:T(8,128)(2,1)} %w_in.1), custom_call_target="tpu_custom_call" | custom-call | flops 4294967296 | bytes 3932160 | tf_op jit(solution)/shard_map/pallas_call | solution.py:207
  127.5 2.1 %copy.6 = bf16[1,128,3072]{2,1,0:T(8,128)(2,1)} copy(bf16[1,128,3072]{2,1,0:T(8,128)(2,1)} %bitcast.4) | data formatting | bytes 1572864

commit v2 on v1

--- a/solution.py
+++ b/solution.py
@@ -24,17 +24,23 @@
     def seq_peer(off):
         return lax.rem(me + off, n)
 
-    def dp_peer(off):
-        return lax.rem(col + off, m)
+    chips = m // 2
+    sibling = col + 1 - 2 * lax.rem(col, 2)
+
+    def w_peer(chip):
+        return lax.rem(col + 2 * chip, m) if chip else sibling
+
+    def w_origin(chip):
+        return lax.rem(col + m - 2 * chip, m) if chip else sibling
 
     barrier = pltpu.get_barrier_semaphore()
     for off in range(1, n):
         pl.semaphore_signal(barrier, inc=1, device_id={"seq": seq_peer(off)},
                             device_id_type=pl.DeviceIdType.MESH)
-    for off in range(1, m):
-        pl.semaphore_signal(barrier, inc=1, device_id={"dp": dp_peer(off)},
+    for chip in range(chips):
+        pl.semaphore_signal(barrier, inc=1, device_id={"dp": w_peer(chip)},
                             device_id_type=pl.DeviceIdType.MESH)
-    pl.semaphore_wait(barrier, n + m - 2)
+    pl.semaphore_wait(barrier, n - 1 + chips)
 
     trio = ((k_in, kb), (v_in, vb), (q_in, qb))
 
@@ -58,23 +64,47 @@
             send_sem=qkv_send.at[t, off], recv_sem=qkv_recv.at[t, off],
             device_id={"seq": seq_peer(1)}, device_id_type=pl.DeviceIdType.MESH)
 
-    def w_copy(off):
+    def w_copy(chip):
         return pltpu.make_async_remote_copy(
             src_ref=w_in, dst_ref=wb.at[col],
-            send_sem=w_send.at[off], recv_sem=w_recv.at[off],
-            device_id={"dp": dp_peer(off)}, device_id_type=pl.DeviceIdType.MESH)
-
-    def w_arrival(off):
-        return pltpu.make_async_remote_copy(
-            src_ref=w_in, dst_ref=wb.at[lax.rem(col + m - off, m)],
-            send_sem=w_send.at[off], recv_sem=w_recv.at[off],
-            device_id={"dp": dp_peer(1)}, device_id_type=pl.DeviceIdType.MESH)
-
-    for t in range(3):
+            send_sem=w_send.at[chip], recv_sem=w_recv.at[chip],
+            device_id={"dp": w_peer(chip)}, device_id_type=pl.DeviceIdType.MESH)
+
+    def w_arrival(chip):
+        return pltpu.make_async_remote_copy(
+            src_ref=w_in, dst_ref=wb.at[w_origin(chip)],
+            send_sem=w_send.at[chip], recv_sem=w_recv.at[chip],
+            device_id={"dp": sibling}, device_id_type=pl.DeviceIdType.MESH)
+
+    def w_pass(chip):
+        return pltpu.make_async_remote_copy(
+            src_ref=wb.at[w_origin(chip)], dst_ref=wb.at[w_origin(chip)],
+            send_sem=w_send.at[chips + chip], recv_sem=w_recv.at[chips + chip],
+            device_id={"dp": sibling}, device_id_type=pl.DeviceIdType.MESH)
+
+    def w_passed(chip):
+        origin = lax.rem(sibling + m - 2 * chip, m)
+        return pltpu.make_async_remote_copy(
+            src_ref=w_in, dst_ref=wb.at[origin],
+            send_sem=w_send.at[chips + chip], recv_sem=w_recv.at[chips + chip],
+            device_id={"dp": sibling}, device_id_type=pl.DeviceIdType.MESH)
+
+    low = jnp.where(me < n // 2, 1, 0)
+
+    def send_queries():
+        for i in range(n):
+            target = jnp.where(low == 1, n - 1 - i, i)
+
+            @pl.when(target != me)
+            def _():
+                qkv_copy(2, lax.rem(target - me + n, n)).start()
+
+    for t in range(2):
         for off in range(1, n):
             qkv_copy(t, off).start()
-    for off in range(1, m):
-        w_copy(off).start()
+    for chip in range(1, chips):
+        w_copy(chip).start()
+    w_copy(0).start()
     own = [pltpu.make_async_copy(trio[t][0].at[:, cols(me)], trio[t][1].at[rows(me)], own_sem.at[t])
            for t in range(3)]
     own.append(pltpu.make_async_copy(w_in, wb.at[col], own_sem.at[3]))
@@ -82,9 +112,14 @@
         copy.start()
     for copy in own:
         copy.wait()
-    for t in range(2):
-        for off in range(1, n):
-            qkv_arrival(t, off).wait_recv()
+    for off in range(1, n):
+        qkv_arrival(0, off).wait_recv()
+    send_queries()
+    for chip in range(1, chips):
+        w_arrival(chip).wait_recv()
+        w_pass(chip).start()
+    for off in range(1, n):
+        qkv_arrival(1, off).wait_recv()
 
     scale = HEAD_DIM ** -0.5 * math.log2(math.e)
 
@@ -118,8 +153,6 @@
             send_sem=sum_send.at[0], recv_sem=sum_recv.at[slot],
             device_id={"seq": seq_peer(1)}, device_id_type=pl.DeviceIdType.MESH)
 
-    low = jnp.where(me < n // 2, 1, 0)
-
     def item(index, carry):
         s = index // 2
         pos = index % 2
@@ -136,8 +169,9 @@
 
             @pl.when(index == 0)
             def _():
-                for off in range(1, m):
-                    w_arrival(off).wait_recv()
+                w_arrival(0).wait_recv()
+                for chip in range(1, chips):
+                    w_passed(chip).wait_recv()
 
             project(dest)
 
@@ -182,8 +216,10 @@
     for t in range(3):
         for off in range(1, n):
             qkv_copy(t, off).wait_send()
-    for off in range(1, m):
-        w_copy(off).wait_send()
+    for chip in range(chips):
+        w_copy(chip).wait_send()
+    for chip in range(1, chips):
+        w_pass(chip).wait_send()
 
     def drain(dest, carry):
         @pl.when(dest != me)

time: 130 us -> 119 us (0.915)
  the two profiles are of different devices: /device:TPU:9 before, /device:TPU:10 now
where the time goes in v2:
time: 119 us
  Pallas kernels  117 us (98%)
  local copies, waits for them, and re-layouts  2.06 us (2%)
    pallas_call x1, Pallas kernels, per_device(): pl.pallas_call(functools.partial(kernel, n, m), out_shape=jax.ShapeDtypeS...  117 us

profile of v2, /device:TPU:10, one launch (start us, length us, event | category | flops | bytes accessed | tf_op | source)
XLA Modules:
  0.0 118.8 jit_solution(12844398358721753195)
XLA Ops:
  0.0 116.7 %shard_map.46 = bf16[128,3072]{1,0:T(8,128)(2,1)} custom-call(bf16[128,4096]{1,0:T(8,128)(2,1)} %bitcast.5, bf16[128,4096]{1,0:T(8,128)(2,1)} %bitcast.6, bf16[128,4096]{1,0:T(8,128)(2,1)} %bitcast.7, bf16[1024,384]{1,0:T(8,128)(2,1)} %w_in.1), custom_call_target="tpu_custom_call" | custom-call | flops 4294967296 | bytes 3932160 | tf_op jit(solution)/shard_map/pallas_call | solution.py:243
  116.7 2.1 %copy.6 = bf16[1,128,3072]{2,1,0:T(8,128)(2,1)} copy(bf16[1,128,3072]{2,1,0:T(8,128)(2,1)} %bitcast.4) | data formatting | bytes 1572864

commit v3 on v2

--- a/solution.py
+++ b/solution.py
@@ -91,20 +91,16 @@
 
     low = jnp.where(me < n // 2, 1, 0)
 
-    def send_queries():
-        for i in range(n):
-            target = jnp.where(low == 1, n - 1 - i, i)
-
-            @pl.when(target != me)
-            def _():
-                qkv_copy(2, lax.rem(target - me + n, n)).start()
-
-    for t in range(2):
-        for off in range(1, n):
-            qkv_copy(t, off).start()
     for chip in range(1, chips):
         w_copy(chip).start()
     w_copy(0).start()
+    for i in range(n):
+        target = jnp.where(low == 1, n - 1 - i, i)
+
+        @pl.when(target != me)
+        def _():
+            for t in range(3):
+                qkv_copy(t, lax.rem(target - me + n, n)).start()
     own = [pltpu.make_async_copy(trio[t][0].at[:, cols(me)], trio[t][1].at[rows(me)], own_sem.at[t])
            for t in range(3)]
     own.append(pltpu.make_async_copy(w_in, wb.at[col], own_sem.at[3]))
@@ -114,7 +110,6 @@
         copy.wait()
     for off in range(1, n):
         qkv_arrival(0, off).wait_recv()
-    send_queries()
     for chip in range(1, chips):
         w_arrival(chip).wait_recv()
         w_pass(chip).start()

time: 119 us -> 114 us (0.958)
  Pallas kernels: 117 us -> 112 us
    pallas_call x1, Pallas kernels: 117 us -> 112 us  [per_device(): pl.pallas_call(functools.partial(kernel, n, m), out_shape=jax.ShapeDtypeS...]
where the time goes in v3:
time: 114 us
  Pallas kernels  112 us (98%)
  local copies, waits for them, and re-layouts  2.06 us (2%)
    pallas_call x1, Pallas kernels, per_device(): pl.pallas_call(functools.partial(kernel, n, m), out_shape=jax.ShapeDtypeS...  112 us

profile of v3, /device:TPU:10, one launch (start us, length us, event | category | flops | bytes accessed | tf_op | source)
XLA Modules:
  0.0 113.8 jit_solution(6371398347927707501)
XLA Ops:
  0.0 111.7 %shard_map.46 = bf16[128,3072]{1,0:T(8,128)(2,1)} custom-call(bf16[128,4096]{1,0:T(8,128)(2,1)} %bitcast.5, bf16[128,4096]{1,0:T(8,128)(2,1)} %bitcast.6, bf16[128,4096]{1,0:T(8,128)(2,1)} %bitcast.7, bf16[1024,384]{1,0:T(8,128)(2,1)} %w_in.1), custom_call_target="tpu_custom_call" | custom-call | flops 4294967296 | bytes 3932160 | tf_op jit(solution)/shard_map/pallas_call | solution.py:238
  111.8 2.1 %copy.6 = bf16[1,128,3072]{2,1,0:T(8,128)(2,1)} copy(bf16[1,128,3072]{2,1,0:T(8,128)(2,1)} %bitcast.4) | data formatting | bytes 1572864

commit v4 on v3

--- a/solution.py
+++ b/solution.py
@@ -129,23 +129,27 @@
             o = jnp.dot(p.astype(jnp.bfloat16), vb[:, c], preferred_element_type=jnp.float32)
             att[:, c] = (o / total).astype(jnp.bfloat16)
 
-    def project(dest):
-        for j in range(m):
+    half = m * wcols // 2
+
+    def project(dest, c):
+        for j in range(c * m // 2, (c + 1) * m // 2):
             part[dest, :, j * wcols:(j + 1) * wcols] = jnp.dot(
                 att[...], wb[j], preferred_element_type=jnp.float32).astype(jnp.bfloat16)
 
-    def sum_copy(dest, up):
+    def sum_copy(dest, up, c):
         target = me + 2 * up - 1
         slot = jnp.where((up == 0) & (target == dest), n, dest)
         return pltpu.make_async_remote_copy(
-            src_ref=part.at[dest], dst_ref=inbox.at[slot],
-            send_sem=sum_send.at[dest], recv_sem=sum_recv.at[slot],
+            src_ref=part.at[dest, :, pl.ds(c * half, half)],
+            dst_ref=inbox.at[slot, :, pl.ds(c * half, half)],
+            send_sem=sum_send.at[dest, c], recv_sem=sum_recv.at[slot, c],
             device_id={"seq": target}, device_id_type=pl.DeviceIdType.MESH)
 
-    def sum_arrival(slot):
-        return pltpu.make_async_remote_copy(
-            src_ref=part.at[0], dst_ref=inbox.at[slot],
-            send_sem=sum_send.at[0], recv_sem=sum_recv.at[slot],
+    def sum_arrival(slot, c):
+        return pltpu.make_async_remote_copy(
+            src_ref=part.at[0, :, pl.ds(c * half, half)],
+            dst_ref=inbox.at[slot, :, pl.ds(c * half, half)],
+            send_sem=sum_send.at[0, c], recv_sem=sum_recv.at[slot, c],
             device_id={"seq": seq_peer(1)}, device_id_type=pl.DeviceIdType.MESH)
 
     def item(index, carry):
@@ -168,45 +172,53 @@
                 for chip in range(1, chips):
                     w_passed(chip).wait_recv()
 
-            project(dest)
-
         active = jnp.where(up == 1, jnp.where(me < dest, 1, 0), jnp.where(me > dest, 1, 0))
         inner = jnp.where(up == 1, jnp.where(me > 0, 1, 0), jnp.where(me < n - 1, 1, 0))
 
-        @pl.when(active == 1)
-        def _():
-            @pl.when(inner == 1)
-            def _():
-                sum_arrival(dest).wait_recv()
-                part[dest] = (part[dest].astype(jnp.float32)
-                              + inbox[dest].astype(jnp.float32)).astype(jnp.bfloat16)
-
-            sum_copy(dest, up).start()
+        for c in range(2):
+            @pl.when(s < (n + 1) // 2)
+            def _():
+                project(dest, c)
+
+            @pl.when(active == 1)
+            def _():
+                @pl.when(inner == 1)
+                def _():
+                    cut = slice(c * half, (c + 1) * half)
+                    sum_arrival(dest, c).wait_recv()
+                    part[dest, :, cut] = (part[dest, :, cut].astype(jnp.float32)
+                                          + inbox[dest, :, cut].astype(jnp.float32)).astype(jnp.bfloat16)
+
+                sum_copy(dest, up, c).start()
 
         return carry
 
     lax.fori_loop(0, 2 * n, item, 0)
 
-    @pl.when(me > 0)
-    def _():
-        sum_arrival(me).wait_recv()
-
-    @pl.when(me < n - 1)
-    def _():
-        sum_arrival(n).wait_recv()
-
-    @pl.when(me == 0)
-    def _():
-        out[...] = (part[me].astype(jnp.float32) + inbox[n].astype(jnp.float32)).astype(jnp.bfloat16)
-
-    @pl.when(me == n - 1)
-    def _():
-        out[...] = (part[me].astype(jnp.float32) + inbox[me].astype(jnp.float32)).astype(jnp.bfloat16)
-
-    @pl.when((me > 0) & (me < n - 1))
-    def _():
-        out[...] = (part[me].astype(jnp.float32) + inbox[me].astype(jnp.float32)
-                    + inbox[n].astype(jnp.float32)).astype(jnp.bfloat16)
+    for c in range(2):
+        cut = slice(c * half, (c + 1) * half)
+        mine = part[me, :, cut].astype(jnp.float32)
+
+        @pl.when(me > 0)
+        def _():
+            sum_arrival(me, c).wait_recv()
+
+        @pl.when(me < n - 1)
+        def _():
+            sum_arrival(n, c).wait_recv()
+
+        @pl.when(me == 0)
+        def _():
+            out[:, cut] = (mine + inbox[n, :, cut].astype(jnp.float32)).astype(jnp.bfloat16)
+
+        @pl.when(me == n - 1)
+        def _():
+            out[:, cut] = (mine + inbox[me, :, cut].astype(jnp.float32)).astype(jnp.bfloat16)
+
+        @pl.when((me > 0) & (me < n - 1))
+        def _():
+            out[:, cut] = (mine + inbox[me, :, cut].astype(jnp.float32)
+                           + inbox[n, :, cut].astype(jnp.float32)).astype(jnp.bfloat16)
 
     for t in range(3):
         for off in range(1, n):
@@ -219,7 +231,8 @@
     def drain(dest, carry):
         @pl.when(dest != me)
         def _():
-            sum_copy(dest, jnp.where(dest > me, 1, 0)).wait_send()
+            for c in range(2):
+                sum_copy(dest, jnp.where(dest > me, 1, 0), c).wait_send()
         return carry
 
     lax.fori_loop(0, n, drain, 0)
@@ -244,7 +257,7 @@
             vmem((length, feats), bf16), vmem((length, feats), bf16), vmem((length, feats), bf16),
             vmem((m, depth, wcols), bf16), vmem((tokens, feats), bf16),
             vmem((n, tokens, dout), bf16), vmem((n + 1, tokens, dout), bf16),
-            dma((4,)), dma((3, n)), dma((3, n)), dma((m,)), dma((m,)), dma((n,)), dma((n + 1,)),
+            dma((4,)), dma((3, n)), dma((3, n)), dma((m,)), dma((m,)), dma((n, 2)), dma((n + 1, 2)),
         ],
         compiler_params=pltpu.CompilerParams(
             collective_id=0, has_side_effects=True, vmem_limit_bytes=56 * 1024 * 1024),

time: 114 us -> 113 us (level)
  no operation moved by 1% of the time
where the time goes in v4:
time: 113 us
  Pallas kernels  111 us (98%)
  local copies, waits for them, and re-layouts  2.06 us (2%)
    pallas_call x1, Pallas kernels, per_device(): pl.pallas_call(functools.partial(kernel, n, m), out_shape=jax.ShapeDtypeS...  111 us

profile of v4, /device:TPU:10, one launch (start us, length us, event | category | flops | bytes accessed | tf_op | source)
XLA Modules:
  0.0 113.2 jit_solution(7894707944844966674)
XLA Ops:
  0.0 111.1 %shard_map.46 = bf16[128,3072]{1,0:T(8,128)(2,1)} custom-call(bf16[128,4096]{1,0:T(8,128)(2,1)} %bitcast.5, bf16[128,4096]{1,0:T(8,128)(2,1)} %bitcast.6, bf16[128,4096]{1,0:T(8,128)(2,1)} %bitcast.7, bf16[1024,384]{1,0:T(8,128)(2,1)} %w_in.1), custom_call_target="tpu_custom_call" | custom-call | flops 4294967296 | bytes 3932160 | tf_op jit(solution)/shard_map/pallas_call | solution.py:251
  111.1 2.1 %copy.6 = bf16[1,128,3072]{2,1,0:T(8,128)(2,1)} copy(bf16[1,128,3072]{2,1,0:T(8,128)(2,1)} %bitcast.4) | data formatting | bytes 1572864
